TPU v7x, 32 devices: a whole 2x2x4 slice. The times are simulated.
32 devices in a mesh: dp: 8 (over y, x, core), tensor: 4 (over z).
Axes of the slice: x: 2, y: 2, z: 4, core: 2. Of those that a mesh axis runs over, the one named last changes fastest.
Arguments:
- tokens: bfloat16 [1024, 4096], P('dp', 'tensor'), may hold values from -6 to 6
- cotangent: bfloat16 [1024, 4096], P('dp', 'tensor'), may hold values from -6 to 6
- expert_ids: int32 [1024, 8], P('dp'), may hold values from 0 to 15, all different within a row; in each aligned block of 128 rows (0 to 127, 128 to 255, ...) at most 96 rows name the same one
- route_weights: float32 [1024, 8], P('dp'), may hold values from 0.1 to 1
- w_gate: bfloat16 [16, 1536, 4096], P('dp', 'tensor'), may hold values from -0.09375 to 0.09375
- w_up: bfloat16 [16, 1536, 4096], P('dp', 'tensor'), may hold values from -0.09375 to 0.09375
Outputs:
- grad_down: bfloat16 [16, 1536, 4096], P('dp', 'tensor')
Inputs may be any that keep to these rules, and one draw needn't show every extreme that they name: `expert_ids`: each row names 8 different experts. Among the 128 rows of one device no expert is named more than 96 times, a bound that some block reaches.
All inputs are finite; a program needn't handle non-finite values.
Results may differ from a plain program's by a relative error of at most 0.0058.
Values may be sent and summed in bfloat16 or wider, within the bound.
A program may use at most 128 MiB of HBM per device.

v0:
```python
import jax
import jax.numpy as jnp
from jax import lax
from jax.sharding import PartitionSpec as P


def build_table(flat_ids, first_expert, held_count, block_count, capacity):
    local_expert = flat_ids - first_expert
    inside = (local_expert >= 0) & (local_expert < held_count)
    onehot = (local_expert[:, :, None] == jnp.arange(held_count)[None, None, :]).astype(jnp.int32)
    slot_index = jnp.sum((jnp.cumsum(onehot, axis=1) - 1) * onehot, axis=2)
    block_index = jnp.arange(block_count)[:, None]
    target = local_expert * (block_count * capacity) + block_index * capacity + slot_index
    target = jnp.where(inside, target, held_count * block_count * capacity)
    pair_index = jnp.arange(flat_ids.shape[0] * flat_ids.shape[1])
    empty_table = jnp.full((held_count * block_count * capacity,), -1, jnp.int32)
    return empty_table.at[target.reshape(-1)].set(pair_index, mode="drop")


def pick_rows(slot_table, token_rows, cot_rows, flat_shares, top_count):
    is_live = slot_table >= 0
    safe_index = jnp.maximum(slot_table, 0)
    token_row = safe_index // top_count
    routed = jnp.where(is_live[:, None], token_rows[token_row], jnp.zeros((), token_rows.dtype))
    weighting = jnp.where(is_live, flat_shares[safe_index], 0.0)
    scaled_rows = (weighting[:, None] * cot_rows[token_row].astype(jnp.float32)).astype(
        jnp.bfloat16
    )
    return (routed, scaled_rows)


def shards(tokens, cotangent, expert_ids, route_weights, w_gate, w_up):
    dp_count = lax.axis_size("dp")
    exp_dev = w_gate.shape[0]
    experts = exp_dev * dp_count
    tok_rows, width_local = tokens.shape
    top_count = expert_ids.shape[1]
    capacity = 3 * tok_rows * top_count // (2 * experts)
    shares = route_weights / jnp.sum(route_weights, axis=1, keepdims=True)
    slot_table = build_table(expert_ids.reshape(1, tok_rows * top_count), 0, experts, 1, capacity)
    routed, scaled_rows = pick_rows(slot_table, tokens, cotangent, shares.reshape(-1), top_count)
    send_rows = routed.reshape(experts, capacity, width_local)
    send_cot = scaled_rows.reshape(experts, capacity, width_local)
    wide_rows = lax.all_gather(send_rows, "tensor", axis=2, tiled=True)
    received, cot_recv = (
        lax.all_to_all(wide_rows, "dp", split_axis=0, concat_axis=1, tiled=True),
        lax.all_to_all(send_cot, "dp", split_axis=0, concat_axis=1, tiled=True),
    )
    gate_proj = jnp.einsum("erd,efd->erf", received, w_gate, preferred_element_type=jnp.float32)
    up_proj = jnp.einsum("erd,efd->erf", received, w_up, preferred_element_type=jnp.float32)
    hidden = (jax.nn.silu(gate_proj) * up_proj).astype(jnp.bfloat16)
    return jnp.einsum(
        "erf,erd->efd",
        hidden,
        lax.all_gather(cot_recv, "tensor", axis=2, tiled=True),
        preferred_element_type=jnp.float32,
    ).astype(jnp.bfloat16)


def solution(mesh):
    placed = (
        P("dp", "tensor"),
        P("dp", "tensor"),
        P("dp", None),
        P("dp", None),
        P("dp", "tensor", None),
        P("dp", "tensor", None),
    )
    return jax.shard_map(
        shards, mesh=mesh, in_specs=placed, out_specs=P("dp", "tensor", None), check_vma=False
    )
```

profile of v0, /device:TPU:0, one launch (start us, length us, event | category | flops | bytes accessed | tf_op | source)
XLA Modules:
  0.0 498.9 jit_solution(14203477950857571594)
XLA Ops:
  6.5 0.8 copy.12
  7.4 0.1 eq.27
  7.5 4.5 reduce-window.6
  12.0 0.1 slice.14
  12.1 0.7 broadcast_multiply_fusion
  12.8 0.7 compare_and_fusion
  13.5 0.1 copy.13
  13.9 0.1 copy.11
  14.0 0.1 mul.42
  14.1 0.1 copy.10
  14.2 0.1 and.22
  14.4 4.3 scatter_custom_fusion
  18.7 0.7 reduce_sum.22
  19.4 0.7 broadcast_divide_fusion
  20.1 0.1 copy.16
  20.2 0.1 reshape.222
  20.3 5.9 %gather_fusion.1 = f32[1536]{0:T(1024)S(1)} fusion(f32[1024]{0:T(1024)S(1)} %reshape.222, s32[2048]{0:T(1024)S(1)} %get-tuple-element.9), kind=kCustom, calls=%fused_computation.1 | custom fusion | bytes 18432 | tf_op jit(solution)/shard_map/gather | solution.py:25
  26.2 0.1 broadcast_in_dim.39
  26.3 5.1 %gather_fusion = bf16[1536,1024]{1,0:T(8,128)(2,1)S(1)} fusion(bf16[128,1024]{1,0:T(8,128)(2,1)S(1)} %copy-done, s32[2048]{0:T(1024)S(1)} %get-tuple-element.10), kind=kCustom, calls=%fused_computation | custom fusion | bytes 6297600 | tf_op jit(solution)/shard_map/gather | solution.py:24
  31.3 1.9 broadcast_select_fusion
  33.4 0.8 copy-done.2
  34.2 5.1 %gather_fusion.2 = bf16[1536,1024]{1,0:T(8,128)(2,1)S(1)} fusion(bf16[128,1024]{1,0:T(8,128)(2,1)S(1)} %copy-done.2, s32[2048]{0:T(1024)S(1)} %get-tuple-element.10), kind=kCustom, calls=%fused_computation.2 | custom fusion | bytes 6297600 | tf_op jit(solution)/shard_map/gather | solution.py:26
  39.3 0.6 fusion
  39.9 42.8 %all_to_all.36 = bf16[16,96,1024]{2,1,0:T(8,128)(2,1)S(1)} all-to-all(bf16[16,96,1024]{2,1,0:T(8,128)(2,1)S(1)} %fusion), channel_id=1, replica_groups=mesh['dp'=8,'tensor'=4] {'dp'}, dimensions={0} | all-to-all | bytes 6291456 | tf_op jit(solution)/shard_map/all_to_all | solution.py:47
  82.7 2.1 copy.17
  84.8 169.6 %all-gather.3.cloned.1.call-done = bf16[16,96,4096]{2,1,0:T(8,128)(2,1)} async-done(((bf16[16,96,1024]{2,1,0:T(8,128)(2,1)}), bf16[16,96,4096]{2,1,0:T(8,128)(2,1)}) %all-gather.3.cloned.1.call-update) | async-done | bytes 12582928 | tf_op jit(solution)/shard_map/all_gather | solution.py:44
  254.4 143.2 %all_to_all.37 = bf16[16,96,4096]{2,1,0:T(8,128)(2,1)S(1)} all-to-all(bf16[16,96,4096]{2,1,0:T(8,128)(2,1)} %all-gather.3.cloned.1.call-done), channel_id=1, replica_groups=mesh['dp'=8,'tensor'=4] {'dp'}, dimensions={0} | all-to-all | bytes 25165824 | tf_op jit(solution)/shard_map/all_to_all | solution.py:46
  397.6 1.9 copy.15
  399.5 4.5 copy-done.3
  404.0 8.1 %fusion.5 = f32[2,768,384]{2,1,0:T(8,128)} fusion(bf16[2,768,4096]{2,1,0:T(8,128)(2,1)S(1)} %bitcast.43, bf16[2,384,4096]{2,1,0:T(8,128)(2,1)S(1)} %bitcast.54), kind=kOutput, calls=%fused_computation.30 | convolution fusion | flops 4831838208 | bytes 21233664 | tf_op jit(solution)/shard_map/erd,efd->erf/dot_general | solution.py:49
  412.1 60.3 %all-gather.5.cloned.1.call-done = bf16[2,768,4096]{2,1,0:T(8,128)(2,1)} async-done(((bf16[2,768,1024]{2,1,0:T(8,128)(2,1)}), bf16[2,768,4096]{2,1,0:T(8,128)(2,1)}) %all-gather.5.cloned.1.call-update) | async-done | bytes 12582928 | tf_op jit(solution)/shard_map/all_gather | solution.py:55
  472.4 19.7 %convolution_convert_fusion = bf16[2,384,4096]{2,1,0:T(8,128)(2,1)} fusion(bf16[2,768,4096]{2,1,0:T(8,128)(2,1)} %all-gather.5.cloned.1.call-done, f32[2,768,384]{2,1,0:T(8,128)} %fusion.5, bf16[2,768,4096]{2,1,0:T(8,128)(2,1)} %bitcast.44, bf16[2,384,4096]{2,1,0:T(8,128)(2,1)} %param.11), kind=kOutput, calls=%fused_computation.4 | convolution fusion | flops 9670361088 | bytes 40108032 | tf_op jit(solution)/shard_map/erf,erd->efd/dot_general | solution.py:52
  (30 shorter events, 0.5 us)
Async XLA Ops:
  6.5 19.7 %copy-start = (bf16[128,1024]{1,0:T(8,128)(2,1)S(1)}, bf16[128,1024]{1,0:T(8,128)(2,1)}, u32[]{:S(2)}) copy-start(bf16[128,1024]{1,0:T(8,128)(2,1)} %param.6) | copy-start | bytes 786436
  6.5 247.8 %all-gather.3.cloned.1.call-start = ((), (), s32[]{:S(2)}) async-start(), calls=%async_computation.2 | async-start | bytes 15728640 | tf_op jit(solution)/shard_map/all_gather | solution.py:44
  33.3 0.9 copy-start.2
  33.3 439.1 %all-gather.5.cloned.1.call-start = ((), (), s32[]{:S(2)}) async-start(), calls=%async_computation.3 | async-start | bytes 15728640 | tf_op jit(solution)/shard_map/all_gather | solution.py:55
  254.4 149.6 %slice-start = ((s8[6291456]{0:T(1024)(128)(4,1)}), s8[4194304]{0:T(1024)(128)(4,1)S(1)}, s32[]{:S(2)}) async-start(s8[6291456]{0:T(1024)(128)(4,1)} %bitcast.53), calls=%async_computation.4 | async-start | bytes 8388608
  397.6 6.4 %slice-start.1 = ((s8[6291456]{0:T(1024)(128)(4,1)}), s8[2097152]{0:T(1024)(128)(4,1)S(1)}, s32[]{:S(2)}) async-start(s8[6291456]{0:T(1024)(128)(4,1)} %bitcast.53), calls=%async_computation.5 | async-start | bytes 4194304
  399.5 4.5 copy-start.3
  472.4 19.7 %copy-start.1 = (bf16[128,1024]{1,0:T(8,128)(2,1)S(1)}, bf16[128,1024]{1,0:T(8,128)(2,1)}, u32[]{:S(2)}) copy-start(bf16[128,1024]{1,0:T(8,128)(2,1)} %param.6) | copy-start | bytes 786436
Sparse Core Ops, SparseCore 0:
  33.4 220.8 all-gather.2
  255.9 216.3 all-gather.4
where the time goes:
time: 499 us
  waiting for transfers between devices  230 us (46%)
  blocking collectives  186 us (37%)
  local copies, waits for them, and re-layouts  31.7 us (6%)
  matrix products  27.8 us (6%)
  between operations  13.5 us (3%)
  other arithmetic  9.92 us (2%)
    all_gather x1, waiting for transfers between devices, shards(): wide_rows = lax.all_gather(send_rows, 'tensor', axis=2, tiled=True)  170 us
    all_to_all x1, blocking collectives, shards(): lax.all_to_all(wide_rows, 'dp', split_axis=0, concat_axis=1, tiled=True)  143 us
    all_gather x1, waiting for transfers between devices, shards(): lax.all_gather(cot_recv, 'tensor', axis=2, tiled=True)  60.3 us
    all_to_all x1, blocking collectives, shards(): lax.all_to_all(send_cot, 'dp', split_axis=0, concat_axis=1, tiled=True)  42.8 us
    dot_general x1, matrix products, shards(): jnp.einsum('erf,erd->efd', hidden, lax.all_gather(cot_recv, 'tensor', axi...  19.7 us
  transfers between devices with their start and end apart: 2, of which 2 were waited for; matrix products, arithmetic and copies ran while one was open for 4% of the time, Pallas kernels for 0%

commit v1 on v0

v1 whole, which is shorter than its diff:
```python
import jax
import jax.numpy as jnp
from jax import lax
from jax.sharding import PartitionSpec as P


def shards(tokens, cotangent, expert_ids, route_weights, w_gate, w_up):
    dp_count = lax.axis_size("dp")
    exp_dev = w_gate.shape[0]
    experts = exp_dev * dp_count
    shares = route_weights / jnp.sum(route_weights, axis=1, keepdims=True)
    onehot = expert_ids[:, :, None] == jnp.arange(experts)[None, None, :]
    dense = jnp.sum(jnp.where(onehot, shares[:, :, None], 0.0), axis=1).T
    rows = lax.all_gather(lax.all_gather(tokens, "tensor", axis=1, tiled=True), "dp", axis=0, tiled=True)
    cots = lax.all_gather(lax.all_gather(cotangent, "tensor", axis=1, tiled=True), "dp", axis=0, tiled=True)
    mine = lax.all_to_all(dense, "dp", split_axis=0, concat_axis=1, tiled=True)
    gate = jnp.einsum("efd,rd->efr", w_gate, rows, preferred_element_type=jnp.float32)
    up = jnp.einsum("efd,rd->efr", w_up, rows, preferred_element_type=jnp.float32)
    hidden = (jax.nn.silu(gate) * up * mine[:, None, :]).astype(jnp.bfloat16)
    return jnp.einsum("efr,rd->efd", hidden, cots, preferred_element_type=jnp.float32).astype(jnp.bfloat16)


def solution(mesh):
    placed = (
        P("dp", "tensor"),
        P("dp", "tensor"),
        P("dp", None),
        P("dp", None),
        P("dp", "tensor", None),
        P("dp", "tensor", None),
    )
    return jax.shard_map(
        shards, mesh=mesh, in_specs=placed, out_specs=P("dp", "tensor", None), check_vma=False
    )
```

time: 499 us -> 199 us (0.40)
  blocking collectives: 186 us -> 0 us
  waiting for transfers between devices: 230 us -> 144 us
  local copies, waits for them, and re-layouts: 31.7 us -> 0 us
  other arithmetic: 9.92 us -> 2.7 us
  matrix products: 27.8 us -> 34.8 us
    all_to_all x2 -> x0, blocking collectives: 186 us -> none  [the longest x1 143 us: shards(): lax.all_to_all(wide_rows, 'dp', split_axis=0, concat_axis=1, tiled=True)]
    all_gather x2 -> x4, waiting for transfers between devices: 230 us -> 142 us  [the longest x1 49.4 us: shards(): lax.all_gather(lax.all_gather(tokens, 'tensor', axis=1, tiled=True), 'dp'...]
    gather x3 -> x0, local copies, waits for them, and re-layouts: 16 us -> none  [the longest x1 5.85 us: pick_rows(): weighting = jnp.where(is_live, flat_shares[safe_index], 0.0)]
    dot_general x2 -> x3, matrix products: 27.8 us -> 34.8 us  [the longest x1 12.6 us: shards(): jnp.einsum('efd,rd->efr', w_gate, rows, preferred_element_type=jnp.float32)]
    unnamed x14 -> x0, local copies, waits for them, and re-layouts: 6.13 us -> none
  transfers between devices with their start and end apart: 2 -> 5, of which waited for: 2 -> 4; matrix products, arithmetic and copies ran while one was open for 4% -> 13% of each run, Pallas kernels for 0% -> 0%
where the time goes in v1:
time: 199 us; the launch traced here: 198 us
  waiting for transfers between devices  144 us (72%)
  matrix products  34.8 us (17%)
  between operations  13.1 us (7%)
  starting transfers between devices  3.77 us (2%)
  other arithmetic  2.7 us (1%)
    all_gather x1, waiting for transfers between devices, shards(): lax.all_gather(lax.all_gather(tokens, 'tensor', axis=1, tiled=True), 'dp'...  49.4 us
    all_gather x1, waiting for transfers between devices, shards(): lax.all_gather(lax.all_gather(cotangent, 'tensor', axis=1, tiled=True), '...  32.6 us
    all_gather x1, waiting for transfers between devices, shards(): lax.all_gather(tokens, 'tensor', axis=1, tiled=True)  31.5 us
    all_gather x1, waiting for transfers between devices, shards(): lax.all_gather(cotangent, 'tensor', axis=1, tiled=True)  29 us
    dot_general x1, matrix products, shards(): jnp.einsum('efd,rd->efr', w_gate, rows, preferred_element_type=jnp.float32)  12.6 us
    dot_general x1, matrix products, shards(): jnp.einsum('efr,rd->efd', hidden, cots, preferred_element_type=jnp.float32)  11.2 us
    dot_general x1, matrix products, shards(): jnp.einsum('efd,rd->efr', w_up, rows, preferred_element_type=jnp.float32)  11 us
  transfers between devices with their start and end apart: 5, of which 4 were waited for; matrix products, arithmetic and copies ran while one was open for 13% of the time, Pallas kernels for 0%

profile of v1, /device:TPU:0, one launch (start us, length us, event | category | flops | bytes accessed | tf_op | source)
XLA Modules:
  0.0 198.3 jit_solution(13856113744473703224)
XLA Ops:
  6.5 0.0 all-gather.5.cloned.1.call-start
  6.5 0.7 all-gather.5.cloned.1.call-update
  7.3 0.0 all-gather.9.cloned.1.call-start
  7.3 0.7 all-gather.9.cloned.1.call-update
  8.0 0.0 all-gather.7.cloned.1.call-start
  8.1 31.5 %all-gather.5.cloned.1.call-done = bf16[128,4096]{1,0:T(8,128)(2,1)} async-done(((bf16[128,1024]{1,0:T(8,128)(2,1)}), bf16[128,4096]{1,0:T(8,128)(2,1)}) %all-gather.5.cloned.1.call-update) | async-done | bytes 1048592 | tf_op jit(solution)/shard_map/all_gather | solution.py:14
  39.6 0.0 all-gather.7.cloned.1.call-update
  39.6 0.0 all-gather.11.cloned.1.call-start
  39.7 29.0 %all-gather.9.cloned.1.call-done = bf16[128,4096]{1,0:T(8,128)(2,1)} async-done(((bf16[128,1024]{1,0:T(8,128)(2,1)}), bf16[128,4096]{1,0:T(8,128)(2,1)}) %all-gather.9.cloned.1.call-update) | async-done | bytes 1048592 | tf_op jit(solution)/shard_map/all_gather | solution.py:15
  68.6 0.0 all-gather.11.cloned.1.call-update
  68.6 0.7 reduce_sum.18
  69.3 0.7 broadcast_divide_fusion
  70.0 1.3 select_reduce_fusion
  71.3 3.7 %all-to-all-start = ((f32[8,2,128]{2,1,0:T(2,128)}), f32[8,2,128]{2,1,0:T(2,128)S(1)}, u32[]{:S(2)}, u32[]{:S(2)}) async-start(f32[8,2,128]{2,1,0:T(2,128)} %bitcast.2), calls=%async_computation | async-start | bytes 16384 | tf_op jit(solution)/shard_map/all_to_all | solution.py:16
  75.0 49.4 %all-gather.7.cloned.1.call-done = bf16[1024,4096]{1,0:T(8,128)(2,1)} async-done(((bf16[128,4096]{1,0:T(8,128)(2,1)}), bf16[1024,4096]{1,0:T(8,128)(2,1)}) %all-gather.7.cloned.1.call-update) | async-done | bytes 8388624 | tf_op jit(solution)/shard_map/all_gather | solution.py:14
  124.4 11.0 %fusion.2 = f32[2,384,1024]{2,1,0:T(8,128)S(1)} fusion(bf16[2,384,4096]{2,1,0:T(8,128)(2,1)} %param.11, bf16[1024,4096]{1,0:T(8,128)(2,1)} %all-gather.7.cloned.1.call-done), kind=kOutput, calls=%fused_computation.2 | convolution fusion | flops 6442450944 | bytes 17825792 | tf_op jit(solution)/shard_map/efd,rd->efr/dot_general | solution.py:18
  135.4 0.0 all-to-all-done
  135.4 12.6 %multiply_convert_fusion = bf16[2,384,1024]{2,1,0:T(8,128)(2,1)} fusion(f32[2,384,1024]{2,1,0:T(8,128)S(1)} %fusion.2, bf16[2,384,4096]{2,1,0:T(8,128)(2,1)} %param.10, bf16[1024,4096]{1,0:T(8,128)(2,1)} %all-gather.7.cloned.1.call-done, f32[2,1024]{1,0:T(2,128)S(1)} %bitcast.21), kind=kOutput, calls=%fused_computation.7 | convolution fusion | flops 6447955968 | bytes 19406848 | tf_op jit(solution)/shard_map/efd,rd->efr/dot_general | solution.py:17
  148.0 32.6 %all-gather.11.cloned.1.call-done = bf16[1024,4096]{1,0:T(8,128)(2,1)} async-done(((bf16[128,4096]{1,0:T(8,128)(2,1)}), bf16[1024,4096]{1,0:T(8,128)(2,1)}) %all-gather.11.cloned.1.call-update) | async-done | bytes 8388624 | tf_op jit(solution)/shard_map/all_gather | solution.py:15
  180.6 11.2 %fusion.6 = bf16[2,384,4096]{2,1,0:T(8,128)(2,1)} fusion(bf16[2,384,1024]{2,1,0:T(8,128)(2,1)} %multiply_convert_fusion, bf16[1024,4096]{1,0:T(8,128)(2,1)} %all-gather.11.cloned.1.call-done), kind=kOutput, calls=%fused_computation.6 | convolution fusion | flops 6445596672 | bytes 16252928 | tf_op jit(solution)/shard_map/efr,rd->efd/dot_general | solution.py:20
Async XLA Ops:
  6.5 33.1 %all-gather.5.cloned.1.call-start = ((), (), s32[]{:S(2)}) async-start(), calls=%async_computation.1 | async-start | bytes 1310720 | tf_op jit(solution)/shard_map/all_gather | solution.py:14
  7.3 61.4 %all-gather.9.cloned.1.call-start = ((), (), s32[]{:S(2)}) async-start(), calls=%async_computation.3 | async-start | bytes 1310720 | tf_op jit(solution)/shard_map/all_gather | solution.py:15
  8.0 116.4 %all-gather.7.cloned.1.call-start = ((), (), s32[]{:S(2)}) async-start(), calls=%async_computation.2 | async-start | bytes 9437184 | tf_op jit(solution)/shard_map/all_gather | solution.py:14
  39.6 141.0 %all-gather.11.cloned.1.call-start = ((), (), s32[]{:S(2)}) async-start(), calls=%async_computation.4 | async-start | bytes 9437184 | tf_op jit(solution)/shard_map/all_gather | solution.py:15
  71.3 64.1 %all-to-all-start = ((f32[8,2,128]{2,1,0:T(2,128)}), f32[8,2,128]{2,1,0:T(2,128)S(1)}, u32[]{:S(2)}, u32[]{:S(2)}) async-start(f32[8,2,128]{2,1,0:T(2,128)} %bitcast.2), calls=%async_computation | async-start | bytes 16384 | tf_op jit(solution)/shard_map/all_to_all | solution.py:16
Sparse Core Ops, SparseCore 0:
  8.9 30.6 all-gather.4
  41.2 27.4 all-gather.8
  70.5 53.8 all-gather.6
  126.2 54.3 all-gather.10

commit v2 on v0

--- a/solution.py
+++ b/solution.py
@@ -1,7 +1,335 @@
+import functools
+
 import jax
 import jax.numpy as jnp
 from jax import lax
+from jax.experimental import pallas as pl
+from jax.experimental.pallas import tpu as pltpu
 from jax.sharding import PartitionSpec as P
+
+MESH = pl.DeviceIdType.MESH
+VMEM_BUDGET = 58 * 1024 * 1024
+UP, DOWN, TO_X, TO_Y, TO_SIB, X_TO_Y, X_SIB, Y_TO_X, Y_SIB, D_LO, D_HI = range(11)
+
+
+def gather_kernel(
+    sizes, tok, cot, ids, weights, w_gate, w_up, out,
+    full, wv, acc, hid, obuf, share_all,
+    send_sem, recv_sem, share_send, share_recv, load_sem, out_sem,
+):
+    dp_count, depth, rows, width, exp_dev, hidden = sizes
+    experts = exp_dev * dp_count
+    total = dp_count * rows
+    held = exp_dev * hidden
+    steps = 2 * depth
+    me, z = lax.axis_index("dp"), lax.axis_index("tensor")
+    core = lax.rem(me, 2)
+    x = lax.rem(lax.div(me, 2), 2)
+    y = lax.div(me, 4)
+    sib = me + 1 - 2 * core
+    xn = me + 2 - 4 * x
+    yn = me + 4 - 8 * y
+    dn = xn + 4 - 8 * y
+    xs, ys, ds = xn + 1 - 2 * core, yn + 1 - 2 * core, dn + 1 - 2 * core
+
+    def block(a, dp, zz, part=None):
+        start, size = dp * rows, rows
+        if part is not None:
+            size = rows // 2
+            start = start + part * size
+        return full.at[
+            a,
+            pl.ds(pl.multiple_of(start, 16), size),
+            pl.ds(pl.multiple_of(zz * width, 128), width),
+        ]
+
+    loads = [
+        pltpu.make_async_copy(tok, block(0, me, z), load_sem.at[0]),
+        pltpu.make_async_copy(cot, block(1, me, z), load_sem.at[1]),
+        pltpu.make_async_copy(w_gate, wv.at[pl.ds(0, held)], load_sem.at[2]),
+        pltpu.make_async_copy(w_up, wv.at[pl.ds(held, held)], load_sem.at[3]),
+    ]
+    for load in loads:
+        load.start()
+
+    barrier = pltpu.get_barrier_semaphore()
+    for p in range(1, dp_count):
+        pl.semaphore_signal(
+            barrier, inc=1, device_id=(lax.rem(me + p, dp_count), z), device_id_type=MESH
+        )
+
+    @pl.when(z > 0)
+    def _():
+        pl.semaphore_signal(barrier, inc=1, device_id=(me, z - 1), device_id_type=MESH)
+
+    @pl.when(z < depth - 1)
+    def _():
+        pl.semaphore_signal(barrier, inc=1, device_id=(me, z + 1), device_id_type=MESH)
+
+    raw = weights[...]
+    share = raw / jnp.sum(raw, axis=0, keepdims=True)
+    named = ids[...]
+    lines = [
+        jnp.sum(jnp.where(named == e, share, 0.0), axis=0, keepdims=True) for e in range(experts)
+    ]
+    share_all[me] = jnp.concatenate(lines, axis=0)
+
+    ends = jnp.where(z > 0, 1, 0) + jnp.where(z < depth - 1, 1, 0)
+    pl.semaphore_wait(barrier, dp_count - 1 + ends)
+
+    def place(k):
+        a = lax.div(k, depth)
+        s = k - a * depth
+        m = jnp.minimum(z, depth - 1 - z)
+        near = jnp.where(lax.rem(s, 2) == 1, z - lax.div(s + 1, 2), z + lax.div(s, 2))
+        far = jnp.where(z == m, s, depth - 1 - s)
+        zz = jnp.where(s <= 2 * m, near, far)
+        return a, zz, a * depth + zz
+
+    def remote(ref, r, kind, dp, zt, at=None):
+        return pltpu.make_async_remote_copy(
+            src_ref=ref,
+            dst_ref=ref,
+            send_sem=send_sem.at[r, kind],
+            recv_sem=recv_sem.at[r, kind if at is None else at],
+            device_id=(dp, zt),
+            device_id_type=MESH,
+        )
+
+    def share_copy(p, dst):
+        return pltpu.make_async_remote_copy(
+            src_ref=share_all.at[me],
+            dst_ref=share_all.at[me],
+            send_sem=share_send.at[p],
+            recv_sem=share_recv.at[p],
+            device_id=(dst, z),
+            device_id_type=MESH,
+        )
+
+    def line_block(k):
+        a, zz, r = place(k)
+        own = block(a, me, zz)
+
+        @pl.when(zz != z)
+        def _():
+            remote(own, r, UP, me, z).wait_recv()
+
+        @pl.when((zz <= z) & (z < depth - 1))
+        def _():
+            remote(own, r, UP, me, z + 1).start()
+
+        @pl.when((zz >= z) & (z > 0))
+        def _():
+            remote(own, r, DOWN, me, z - 1, UP).start()
+
+        remote(own, r, TO_X, xn, z).start()
+        remote(own, r, TO_Y, yn, z).start()
+        remote(own, r, TO_SIB, sib, z).start()
+
+    def neighbour_blocks(k):
+        a, zz, r = place(k)
+        remote(block(a, xn, zz), r, TO_X, xn, z).wait_recv()
+        remote(block(a, xn, zz, 0), r, X_TO_Y, yn, z).start()
+        remote(block(a, xn, zz), r, X_SIB, sib, z).start()
+        remote(block(a, yn, zz), r, TO_Y, yn, z).wait_recv()
+        remote(block(a, yn, zz, 1), r, Y_TO_X, xn, z).start()
+        remote(block(a, yn, zz), r, Y_SIB, sib, z).start()
+
+    def diagonal_blocks(k):
+        a, zz, r = place(k)
+        remote(block(a, dn, zz, 0), r, X_TO_Y, yn, z).wait_recv()
+        remote(block(a, dn, zz, 0), r, D_LO, sib, z).start()
+        remote(block(a, dn, zz, 1), r, Y_TO_X, xn, z).wait_recv()
+        remote(block(a, dn, zz, 1), r, D_HI, sib, z).start()
+
+    def sibling_blocks(k):
+        a, zz, r = place(k)
+        remote(block(a, sib, zz), r, TO_SIB, sib, z).wait_recv()
+        remote(block(a, xs, zz), r, X_SIB, sib, z).wait_recv()
+        remote(block(a, ys, zz), r, Y_SIB, sib, z).wait_recv()
+        remote(block(a, ds, zz, 0), r, D_LO, sib, z).wait_recv()
+        remote(block(a, ds, zz, 1), r, D_HI, sib, z).wait_recv()
+
+    def sent(k):
+        a, zz, r = place(k)
+        own = block(a, me, zz)
+
+        @pl.when((zz <= z) & (z < depth - 1))
+        def _():
+            remote(own, r, UP, me, z + 1).wait_send()
+
+        @pl.when((zz >= z) & (z > 0))
+        def _():
+            remote(own, r, DOWN, me, z - 1, UP).wait_send()
+
+        remote(own, r, TO_X, xn, z).wait_send()
+        remote(own, r, TO_Y, yn, z).wait_send()
+        remote(own, r, TO_SIB, sib, z).wait_send()
+        remote(block(a, xn, zz, 0), r, X_TO_Y, yn, z).wait_send()
+        remote(block(a, xn, zz), r, X_SIB, sib, z).wait_send()
+        remote(block(a, yn, zz, 1), r, Y_TO_X, xn, z).wait_send()
+        remote(block(a, yn, zz), r, Y_SIB, sib, z).wait_send()
+        remote(block(a, dn, zz, 0), r, D_LO, sib, z).wait_send()
+        remote(block(a, dn, zz, 1), r, D_HI, sib, z).wait_send()
+
+    tile = 256
+
+    def project(k):
+        _, zz, _ = place(k)
+        cols = pl.ds(pl.multiple_of(zz * width, 128), width)
+        for g in range(2):
+            @pl.loop(0, total // tile)
+            def _(i):
+                at = pl.ds(pl.multiple_of(i * tile, tile), tile)
+                part = lax.dot_general(
+                    wv[pl.ds(g * held, held), cols],
+                    full[0, at, cols],
+                    (((1,), (1,)), ((), ())),
+                    preferred_element_type=jnp.float32,
+                )
+
+                @pl.when(k == 0)
+                def _():
+                    acc[pl.ds(g * held, held), at] = part
+
+                @pl.when(k > 0)
+                def _():
+                    acc[pl.ds(g * held, held), at] += part
+
+    def activate():
+        for p in range(1, dp_count):
+            src = lax.rem(me + dp_count - p, dp_count)
+            pltpu.make_async_remote_copy(
+                src_ref=share_all.at[src],
+                dst_ref=share_all.at[src],
+                send_sem=share_send.at[p],
+                recv_sem=share_recv.at[p],
+                device_id=(src, z),
+                device_id_type=MESH,
+            ).wait_recv()
+
+        @pl.loop(0, dp_count)
+        def _(p):
+            at = pl.ds(pl.multiple_of(p * rows, 128), rows)
+            for e in range(exp_dev):
+                gate = acc[pl.ds(e * hidden, hidden), at]
+                up = acc[pl.ds(held + e * hidden, hidden), at]
+                line = share_all[p, pl.ds(me * exp_dev + e, 1), :]
+                value = gate / (1.0 + jnp.exp(-gate)) * up * line
+                hid[pl.ds(e * hidden, hidden), at] = value.astype(hid.dtype)
+
+    def store(k):
+        _, zz, _ = place(k)
+        cols = pl.ds(pl.multiple_of(zz * width, 128), width)
+        return pltpu.make_async_copy(obuf.at[:, cols], out.at[:, cols], out_sem.at[zz])
+
+    def down(k):
+        _, zz, _ = place(k)
+
+        @pl.loop(0, width // tile)
+        def _(i):
+            at = pl.ds(pl.multiple_of(zz * width + i * tile, tile), tile)
+            obuf[:, at] = jnp.dot(
+                hid[...], full[1, :, at], preferred_element_type=jnp.float32
+            ).astype(obuf.dtype)
+
+        store(k).start()
+
+    loads[0].wait()
+    loads[1].wait()
+    line_block(0)
+    for p in range(1, dp_count):
+        share_copy(p, lax.rem(me + p, dp_count)).start()
+    line_block(1)
+    neighbour_blocks(0)
+    loads[2].wait()
+    loads[3].wait()
+
+    @pl.loop(0, steps)
+    def _(k):
+        @pl.when(k + 2 < steps)
+        def _():
+            line_block(k + 2)
+
+        @pl.when(k + 1 < steps)
+        def _():
+            neighbour_blocks(k + 1)
+
+        diagonal_blocks(k)
+        sibling_blocks(k)
+
+        @pl.when(k < depth)
+        def _():
+            project(k)
+
+        @pl.when(k == depth - 1)
+        def _():
+            activate()
+
+        @pl.when(k >= depth)
+        def _():
+            down(k)
+
+    @pl.loop(0, steps)
+    def _(k):
+        sent(k)
+
+    for p in range(1, dp_count):
+        share_copy(p, lax.rem(me + p, dp_count)).wait_send()
+
+    @pl.loop(depth, steps)
+    def _(k):
+        store(k).wait()
+
+
+def scratch_bytes(dp_count, depth, rows, width, exp_dev, hidden):
+    total, model, held = dp_count * rows, depth * width, exp_dev * hidden
+    return 4 * total * model + 4 * held * model + 8 * held * total + 2 * held * (total + model)
+
+
+def gather_plan(sizes, tokens, cotangent, expert_ids, route_weights, w_gate, w_up):
+    dp_count, depth, rows, width, exp_dev, hidden = sizes
+    total, model, held = dp_count * rows, depth * width, exp_dev * hidden
+    experts = exp_dev * dp_count
+    steps = 2 * depth
+    hbm = pl.BlockSpec(memory_space=pl.ANY)
+    vmem = pl.BlockSpec(memory_space=pltpu.VMEM)
+    grad = pl.pallas_call(
+        functools.partial(gather_kernel, sizes),
+        out_shape=jax.ShapeDtypeStruct((held, model), jnp.bfloat16),
+        in_specs=[hbm, hbm, vmem, vmem, hbm, hbm],
+        out_specs=hbm,
+        scratch_shapes=[
+            pltpu.VMEM((2, total, model), jnp.bfloat16),
+            pltpu.VMEM((2 * held, model), jnp.bfloat16),
+            pltpu.VMEM((2 * held, total), jnp.float32),
+            pltpu.VMEM((held, total), jnp.bfloat16),
+            pltpu.VMEM((held, model), jnp.bfloat16),
+            pltpu.VMEM((dp_count, experts, rows), jnp.float32),
+            pltpu.SemaphoreType.DMA((steps, 11)),
+            pltpu.SemaphoreType.DMA((steps, 11)),
+            pltpu.SemaphoreType.DMA((dp_count,)),
+            pltpu.SemaphoreType.DMA((dp_count,)),
+            pltpu.SemaphoreType.DMA((4,)),
+            pltpu.SemaphoreType.DMA((depth,)),
+        ],
+        compiler_params=pltpu.CompilerParams(
+            collective_id=0, has_side_effects=True, vmem_limit_bytes=VMEM_BUDGET
+        ),
+        cost_estimate=pl.CostEstimate(
+            flops=6 * held * total * model,
+            bytes_accessed=6 * held * model + 4 * rows * width,
+            transcendentals=held * total,
+        ),
+    )(
+        tokens,
+        cotangent,
+        expert_ids.T,
+        route_weights.T,
+        w_gate.reshape(held, model),
+        w_up.reshape(held, model),
+    )
+    return grad.reshape(exp_dev, hidden, model)
 
 
 def build_table(flat_ids, first_expert, held_count, block_count, capacity):
@@ -29,7 +357,7 @@
     return (routed, scaled_rows)
 
 
-def shards(tokens, cotangent, expert_ids, route_weights, w_gate, w_up):
+def routed_plan(tokens, cotangent, expert_ids, route_weights, w_gate, w_up):
     dp_count = lax.axis_size("dp")
     exp_dev = w_gate.shape[0]
     experts = exp_dev * dp_count
@@ -57,6 +385,14 @@
     ).astype(jnp.bfloat16)
 
 
+def shards(tokens, cotangent, expert_ids, route_weights, w_gate, w_up):
+    dp_count, depth = lax.axis_size("dp"), lax.axis_size("tensor")
+    sizes = (dp_count, depth) + tokens.shape + w_gate.shape[:2]
+    if dp_count == 8 and scratch_bytes(*sizes) < VMEM_BUDGET * 9 // 10:
+        return gather_plan(sizes, tokens, cotangent, expert_ids, route_weights, w_gate, w_up)
+    return routed_plan(tokens, cotangent, expert_ids, route_weights, w_gate, w_up)
+
+
 def solution(mesh):
     placed = (
         P("dp", "tensor"),

time: 499 us -> 105 us (0.21)
  waiting for transfers between devices: 230 us -> 0 us
  blocking collectives: 186 us -> 0 us
  Pallas kernels: 0 us -> 98 us
  matrix products: 27.8 us -> 0 us
  local copies, waits for them, and re-layouts: 31.7 us -> 6.29 us
  between operations: 13.5 us -> 0.01 us
  other arithmetic: 9.92 us -> 0 us
    all_gather x2 -> x0, waiting for transfers between devices: 230 us -> none  [the longest x1 170 us: shards(): wide_rows = lax.all_gather(send_rows, 'tensor', axis=2, tiled=True)]
    all_to_all x2 -> x0, blocking collectives: 186 us -> none  [the longest x1 143 us: shards(): lax.all_to_all(wide_rows, 'dp', split_axis=0, concat_axis=1, tiled=True)]
    pallas_call x0 -> x1, Pallas kernels: none -> 98 us  [gather_plan(): pl.pallas_call(functools.partial(gather_kernel, sizes), out_shape=jax.Sha...]
    dot_general x2 -> x0, matrix products: 27.8 us -> none  [the longest x1 19.7 us: shards(): jnp.einsum('erf,erd->efd', hidden, lax.all_gather(cot_recv, 'tensor', axi...]
    gather x3 -> x0, local copies, waits for them, and re-layouts: 16 us -> none  [the longest x1 5.85 us: pick_rows(): weighting = jnp.where(is_live, flat_shares[safe_index], 0.0)]
  transfers between devices with their start and end apart: 2 -> 0, of which waited for: 2 -> 0; matrix products, arithmetic and copies ran while one was open for 4% -> 0% of each run, Pallas kernels for 0% -> 0%
where the time goes in v2:
time: 105 us; the launch traced here: 104 us
  Pallas kernels  98 us (93%)
  local copies, waits for them, and re-layouts  6.29 us (6%)
    pallas_call x1, Pallas kernels, gather_plan(): pl.pallas_call(functools.partial(gather_kernel, sizes), out_shape=jax.Sha...  98 us
    unnamed x1, local copies, waits for them, and re-layouts  6.29 us

profile of v2, /device:TPU:0, one launch (start us, length us, event | category | flops | bytes accessed | tf_op | source)
XLA Modules:
  0.0 104.3 jit_solution(8147496906303444971)
XLA Ops:
  0.0 98.0 %shard_map.64 = bf16[768,4096]{1,0:T(8,128)(2,1)} custom-call(bf16[128,1024]{1,0:T(8,128)(2,1)} %tok.1, bf16[128,1024]{1,0:T(8,128)(2,1)} %cot.1, s32[8,128]{1,0:T(8,128)} %bitcast.8, f32[8,128]{1,0:T(8,128)} %bitcast.9, bf16[768,4096]{1,0:T(8,128)(2,1)} %bitcast.6, bf16[768,4096]{1,0:T(8,128)(2,1)} %bitcast.7), custom_call_target="tpu_custom_call" | custom-call | flops 19327352832 | bytes 19398656 | tf_op jit(solution)/shard_map/pallas_call | solution.py:297
  98.0 6.3 %copy.8 = bf16[2,384,4096]{2,1,0:T(8,128)(2,1)} copy(bf16[2,384,4096]{2,1,0:T(8,128)(2,1)} %bitcast.5) | data formatting | bytes 12582912

commit v3 on v2

--- a/solution.py
+++ b/solution.py
@@ -9,7 +9,8 @@
 
 MESH = pl.DeviceIdType.MESH
 VMEM_BUDGET = 58 * 1024 * 1024
-UP, DOWN, TO_X, TO_Y, TO_SIB, X_TO_Y, X_SIB, Y_TO_X, Y_SIB, D_LO, D_HI = range(11)
+UP, DOWN, TO_X, TO_Y, TO_SIB, X_TO_Y, X_SIB, Y_TO_X, Y_SIB, D_LO, D_HI, DZ_UP, DZ_DOWN = range(13)
+KINDS = 13
 
 
 def gather_kernel(
@@ -32,11 +33,14 @@
     dn = xn + 4 - 8 * y
     xs, ys, ds = xn + 1 - 2 * core, yn + 1 - 2 * core, dn + 1 - 2 * core
 
+    half, quarter = rows // 2, rows // 4
+    lo, hi = (0, half), (half, half)
+    lo_first, lo_second = (0, quarter), (quarter, quarter)
+
     def block(a, dp, zz, part=None):
         start, size = dp * rows, rows
         if part is not None:
-            size = rows // 2
-            start = start + part * size
+            start, size = start + part[0], part[1]
         return full.at[
             a,
             pl.ds(pl.multiple_of(start, 16), size),
@@ -126,29 +130,62 @@
         remote(own, r, TO_Y, yn, z).start()
         remote(own, r, TO_SIB, sib, z).start()
 
+    def corner_start(a, zz, r, dp, kind, dst, near_part, far_part):
+        @pl.when(zz == z)
+        def _():
+            remote(block(a, dp, zz, near_part), r, kind, dst, z).start()
+
+        @pl.when(zz != z)
+        def _():
+            remote(block(a, dp, zz, far_part), r, kind, dst, z).start()
+
     def neighbour_blocks(k):
         a, zz, r = place(k)
         remote(block(a, xn, zz), r, TO_X, xn, z).wait_recv()
-        remote(block(a, xn, zz, 0), r, X_TO_Y, yn, z).start()
+        corner_start(a, zz, r, xn, X_TO_Y, yn, lo, lo_first)
         remote(block(a, xn, zz), r, X_SIB, sib, z).start()
         remote(block(a, yn, zz), r, TO_Y, yn, z).wait_recv()
-        remote(block(a, yn, zz, 1), r, Y_TO_X, xn, z).start()
+        corner_start(a, zz, r, yn, Y_TO_X, xn, hi, lo_second)
         remote(block(a, yn, zz), r, Y_SIB, sib, z).start()
 
     def diagonal_blocks(k):
         a, zz, r = place(k)
-        remote(block(a, dn, zz, 0), r, X_TO_Y, yn, z).wait_recv()
-        remote(block(a, dn, zz, 0), r, D_LO, sib, z).start()
-        remote(block(a, dn, zz, 1), r, Y_TO_X, xn, z).wait_recv()
-        remote(block(a, dn, zz, 1), r, D_HI, sib, z).start()
+
+        @pl.when(zz == z)
+        def _():
+            remote(block(a, dn, zz, lo), r, X_TO_Y, yn, z).wait_recv()
+            remote(block(a, dn, zz, hi), r, Y_TO_X, xn, z).wait_recv()
+
+        @pl.when(zz != z)
+        def _():
+            remote(block(a, dn, zz, hi), r, DZ_UP, me, z).wait_recv()
+
+        corner = block(a, dn, zz, hi)
+
+        @pl.when((zz <= z) & (z < depth - 1))
+        def _():
+            remote(corner, r, DZ_UP, me, z + 1).start()
+
+        @pl.when((zz >= z) & (z > 0))
+        def _():
+            remote(corner, r, DZ_DOWN, me, z - 1, DZ_UP).start()
+
+        remote(corner, r, D_HI, sib, z).start()
+
+        @pl.when(zz != z)
+        def _():
+            remote(block(a, dn, zz, lo_first), r, X_TO_Y, yn, z).wait_recv()
+            remote(block(a, dn, zz, lo_second), r, Y_TO_X, xn, z).wait_recv()
+
+        remote(block(a, dn, zz, lo), r, D_LO, sib, z).start()
 
     def sibling_blocks(k):
         a, zz, r = place(k)
         remote(block(a, sib, zz), r, TO_SIB, sib, z).wait_recv()
         remote(block(a, xs, zz), r, X_SIB, sib, z).wait_recv()
         remote(block(a, ys, zz), r, Y_SIB, sib, z).wait_recv()
-        remote(block(a, ds, zz, 0), r, D_LO, sib, z).wait_recv()
-        remote(block(a, ds, zz, 1), r, D_HI, sib, z).wait_recv()
+        remote(block(a, ds, zz, lo), r, D_LO, sib, z).wait_recv()
+        remote(block(a, ds, zz, hi), r, D_HI, sib, z).wait_recv()
 
     def sent(k):
         a, zz, r = place(k)
@@ -165,12 +202,29 @@
         remote(own, r, TO_X, xn, z).wait_send()
         remote(own, r, TO_Y, yn, z).wait_send()
         remote(own, r, TO_SIB, sib, z).wait_send()
-        remote(block(a, xn, zz, 0), r, X_TO_Y, yn, z).wait_send()
         remote(block(a, xn, zz), r, X_SIB, sib, z).wait_send()
-        remote(block(a, yn, zz, 1), r, Y_TO_X, xn, z).wait_send()
         remote(block(a, yn, zz), r, Y_SIB, sib, z).wait_send()
-        remote(block(a, dn, zz, 0), r, D_LO, sib, z).wait_send()
-        remote(block(a, dn, zz, 1), r, D_HI, sib, z).wait_send()
+        remote(block(a, dn, zz, lo), r, D_LO, sib, z).wait_send()
+        corner = block(a, dn, zz, hi)
+        remote(corner, r, D_HI, sib, z).wait_send()
+
+        @pl.when(zz == z)
+        def _():
+            remote(block(a, xn, zz, lo), r, X_TO_Y, yn, z).wait_send()
+            remote(block(a, yn, zz, hi), r, Y_TO_X, xn, z).wait_send()
+
+        @pl.when(zz != z)
+        def _():
+            remote(block(a, xn, zz, lo_first), r, X_TO_Y, yn, z).wait_send()
+            remote(block(a, yn, zz, lo_second), r, Y_TO_X, xn, z).wait_send()
+
+        @pl.when((zz <= z) & (z < depth - 1))
+        def _():
+            remote(corner, r, DZ_UP, me, z + 1).wait_send()
+
+        @pl.when((zz >= z) & (z > 0))
+        def _():
+            remote(corner, r, DZ_DOWN, me, z - 1, DZ_UP).wait_send()
 
     tile = 256
 
@@ -242,20 +296,26 @@
         share_copy(p, lax.rem(me + p, dp_count)).start()
     line_block(1)
     neighbour_blocks(0)
+    line_block(2)
+    neighbour_blocks(1)
+    diagonal_blocks(0)
     loads[2].wait()
     loads[3].wait()
 
     @pl.loop(0, steps)
     def _(k):
+        @pl.when(k + 3 < steps)
+        def _():
+            line_block(k + 3)
+
         @pl.when(k + 2 < steps)
         def _():
-            line_block(k + 2)
+            neighbour_blocks(k + 2)
 
         @pl.when(k + 1 < steps)
         def _():
-            neighbour_blocks(k + 1)
-
-        diagonal_blocks(k)
+            diagonal_blocks(k + 1)
+
         sibling_blocks(k)
 
         @pl.when(k < depth)
@@ -306,8 +366,8 @@
             pltpu.VMEM((held, total), jnp.bfloat16),
             pltpu.VMEM((held, model), jnp.bfloat16),
             pltpu.VMEM((dp_count, experts, rows), jnp.float32),
-            pltpu.SemaphoreType.DMA((steps, 11)),
-            pltpu.SemaphoreType.DMA((steps, 11)),
+            pltpu.SemaphoreType.DMA((steps, KINDS)),
+            pltpu.SemaphoreType.DMA((steps, KINDS)),
             pltpu.SemaphoreType.DMA((dp_count,)),
             pltpu.SemaphoreType.DMA((dp_count,)),
             pltpu.SemaphoreType.DMA((4,)),

time: 105 us -> 90.5 us (0.86)
  Pallas kernels: 98 us -> 83.9 us
    pallas_call x1, Pallas kernels: 98 us -> 83.9 us  [gather_plan(): pl.pallas_call(functools.partial(gather_kernel, sizes), out_shape=jax.Sha...]
where the time goes in v3:
time: 90.5 us; the launch traced here: 90.2 us
  Pallas kernels  83.9 us (93%)
  local copies, waits for them, and re-layouts  6.29 us (7%)
    pallas_call x1, Pallas kernels, gather_plan(): pl.pallas_call(functools.partial(gather_kernel, sizes), out_shape=jax.Sha...  83.9 us
    unnamed x1, local copies, waits for them, and re-layouts  6.29 us

profile of v3, /device:TPU:0, one launch (start us, length us, event | category | flops | bytes accessed | tf_op | source)
XLA Modules:
  0.0 90.2 jit_solution(12521659933439591695)
XLA Ops:
  0.0 83.9 %shard_map.64 = bf16[768,4096]{1,0:T(8,128)(2,1)} custom-call(bf16[128,1024]{1,0:T(8,128)(2,1)} %tok.1, bf16[128,1024]{1,0:T(8,128)(2,1)} %cot.1, s32[8,128]{1,0:T(8,128)} %bitcast.8, f32[8,128]{1,0:T(8,128)} %bitcast.9, bf16[768,4096]{1,0:T(8,128)(2,1)} %bitcast.6, bf16[768,4096]{1,0:T(8,128)(2,1)} %bitcast.7), custom_call_target="tpu_custom_call" | custom-call | flops 19327352832 | bytes 19398656 | tf_op jit(solution)/shard_map/pallas_call | solution.py:357
  83.9 6.3 %copy.8 = bf16[2,384,4096]{2,1,0:T(8,128)(2,1)} copy(bf16[2,384,4096]{2,1,0:T(8,128)(2,1)} %bitcast.5) | data formatting | bytes 12582912

commit v4 on v3

--- a/solution.py
+++ b/solution.py
@@ -1,4 +1,5 @@
 import functools
+import math
 
 import jax
 import jax.numpy as jnp
@@ -226,7 +227,7 @@
         def _():
             remote(corner, r, DZ_DOWN, me, z - 1, DZ_UP).wait_send()
 
-    tile = 256
+    tile = math.gcd(total, width)
 
     def project(k):
         _, zz, _ = place(k)

time: 90.5 us -> 87.2 us (0.964)
  Pallas kernels: 83.9 us -> 80.7 us
    pallas_call x1, Pallas kernels: 83.9 us -> 80.7 us  [gather_plan(): pl.pallas_call(functools.partial(gather_kernel, sizes), out_shape=jax.Sha...]
where the time goes in v4:
time: 87.2 us; the launch traced here: 87 us
  Pallas kernels  80.7 us (93%)
  local copies, waits for them, and re-layouts  6.29 us (7%)
    pallas_call x1, Pallas kernels, gather_plan(): pl.pallas_call(functools.partial(gather_kernel, sizes), out_shape=jax.Sha...  80.7 us
    unnamed x1, local copies, waits for them, and re-layouts  6.29 us

profile of v4, /device:TPU:0, one launch (start us, length us, event | category | flops | bytes accessed | tf_op | source)
XLA Modules:
  0.0 87.0 jit_solution(13649785211814542543)
XLA Ops:
  0.0 80.7 %shard_map.64 = bf16[768,4096]{1,0:T(8,128)(2,1)} custom-call(bf16[128,1024]{1,0:T(8,128)(2,1)} %tok.1, bf16[128,1024]{1,0:T(8,128)(2,1)} %cot.1, s32[8,128]{1,0:T(8,128)} %bitcast.8, f32[8,128]{1,0:T(8,128)} %bitcast.9, bf16[768,4096]{1,0:T(8,128)(2,1)} %bitcast.6, bf16[768,4096]{1,0:T(8,128)(2,1)} %bitcast.7), custom_call_target="tpu_custom_call" | custom-call | flops 19327352832 | bytes 19398656 | tf_op jit(solution)/shard_map/pallas_call | solution.py:358
  80.7 6.3 %copy.8 = bf16[2,384,4096]{2,1,0:T(8,128)(2,1)} copy(bf16[2,384,4096]{2,1,0:T(8,128)(2,1)} %bitcast.5) | data formatting | bytes 12582912
